TPU v7x, 1024 devices: a whole 8x8x8 slice. The times are simulated.
1024 devices in a mesh: group: 8 (over x_lo, core), node: 16 (over x_hi, y), chip: 8 (over z).
Axes of the slice: x: 8 (x_hi: 2, x_lo: 4; x = x_hi * 4 + x_lo), y: 8, z: 8, core: 2. Of those that a mesh axis runs over, the one named last changes fastest.
Arguments:
- prompt_cache: bfloat16 [8, 16, 4, 192, 576], P('group', 'node', None, 'chip'), may hold values from -4 to 4
- prompt_lengths: int32 [8, 16, 4], replicated, may hold values from 1 to 192, 480 in all within a row
- prompt_replica: int32 [8, 16, 4], replicated, may hold values from 0 to 15, as said below
- new_queries: bfloat16 [8, 16, 16, 2, 128, 576], P('group', 'node', None, None, 'chip'), may hold values from -32 to 32
- new_rows: bfloat16 [8, 16, 16, 2, 576], P('group', 'node'), may hold values from -4 to 4
- resident_cache: bfloat16 [8, 16, 3, 1024, 576], P('group', 'node'), may hold values from -4 to 4
- resident_queries: bfloat16 [8, 16, 3, 2, 128, 576], P('group', 'node', None, None, 'chip'), may hold values from -32 to 32
- resident_rows: bfloat16 [8, 16, 3, 2, 576], P('group', 'node'), may hold values from -4 to 4
- resident_lengths: int32 [8, 16, 3], P('group', 'node'), may hold values from 1 to 1024, 1920 in all within a row
Outputs:
- new_context: bfloat16 [8, 16, 16, 2, 128, 512], P('group', 'node', None, None, 'chip')
- resident_context: bfloat16 [8, 16, 3, 2, 128, 512], P('group', 'node', None, None, 'chip')
Inputs may be any that keep to these rules, and one draw needn't show every extreme that they name: `prompt_replica`: the 4 prompts of one prefill node go to different replicas; one replica may receive prompts from any number of prefill nodes.
All inputs are finite; a program needn't handle non-finite values.
Results may differ from a plain program's by a relative error of at most 0.0034.
Values may be sent and summed in bfloat16 or wider, within the bound.
No kernel may reach another device: no remote copies, remote signals or barrier semaphores. Data moves between devices by JAX's collectives and lax.ppermute only.
A program may use at most 64 MiB of HBM per device.

v0:
```python
import jax
import jax.numpy as jnp
from jax import lax
from jax.sharding import PartitionSpec as P

LATENT = 512


score_scale = 1.0 / 192.0**0.5


def from_behind(value, axis, steps):
    count = lax.axis_size(axis)
    pairs = [(source, (source + steps) % count) for source in range(count)]
    return lax.ppermute(value, axis, pairs)


def key_scores(queries, keys_block):
    return (
        jnp.einsum("bshc,blc->bshl", queries, keys_block, preferred_element_type=jnp.float32)
        * score_scale
    )


def masks_for(keys_cache, own_rows, lengths):
    cache_pos = lax.broadcasted_iota(jnp.int32, (1, 1, 1, keys_cache.shape[1]), 3)
    cache_ok = cache_pos < lengths[:, None, None, None]
    step_count = own_rows.shape[1]
    step_here = lax.broadcasted_iota(jnp.int32, (1, step_count, 1, step_count), 1)
    own_here = lax.broadcasted_iota(jnp.int32, (1, step_count, 1, step_count), 3)
    return (cache_ok, own_here <= step_here)


def weigh(cache_scores, own_scores, row_top, keys_cache, own_rows):
    cache_exp = jnp.exp(cache_scores - row_top[..., None])
    own_exp = jnp.exp(own_scores - row_top[..., None])
    row_total = jnp.sum(cache_exp, axis=3) + jnp.sum(own_exp, axis=3)
    numerator = jnp.einsum(
        "bshl,bld->bshd",
        cache_exp.astype(jnp.bfloat16),
        keys_cache[:, :, :LATENT],
        preferred_element_type=jnp.float32,
    )
    numerator = numerator + jnp.einsum(
        "bshl,bld->bshd",
        own_exp.astype(jnp.bfloat16),
        own_rows[:, :, :LATENT],
        preferred_element_type=jnp.float32,
    )
    return (numerator, row_total)


def attend(queries, keys_cache, own_rows, lengths):
    cache_ok, own_ok = masks_for(keys_cache, own_rows, lengths)
    cache_scores = jnp.where(cache_ok, key_scores(queries, keys_cache), -jnp.inf)
    own_scores = jnp.where(own_ok, key_scores(queries, own_rows), -jnp.inf)
    row_top = jnp.maximum(jnp.max(cache_scores, axis=3), jnp.max(own_scores, axis=3))
    return weigh(cache_scores, own_scores, row_top, keys_cache, own_rows)


def on_device(
    prompt_cache,
    prompt_lengths,
    prompt_replica,
    new_queries,
    new_rows,
    resident_cache,
    resident_queries,
    resident_rows,
    resident_lengths,
):
    group_count = lax.axis_size("group")
    node_count = lax.axis_size("node")
    group_here = lax.axis_index("group")
    node_here = lax.axis_index("node")
    prompt_blocks = prompt_cache[0, 0]
    prompt_count = prompt_blocks.shape[0]
    source_group = (group_here + group_count - group_count // 2) % group_count
    source_table = lax.dynamic_index_in_dim(prompt_replica, source_group, 0, keepdims=False)
    source_lengths = lax.dynamic_index_in_dim(prompt_lengths, source_group, 0, keepdims=False)
    chosen = source_table == node_here
    is_live = jnp.any(chosen, axis=1)
    slot_lengths = jnp.sum(jnp.where(chosen, source_lengths, 0), axis=1)
    own_table = lax.dynamic_index_in_dim(
        lax.dynamic_index_in_dim(prompt_replica, group_here, 0, keepdims=False),
        node_here,
        0,
        keepdims=False,
    )
    replica_ids = lax.broadcasted_iota(jnp.int32, (node_count, prompt_count), 0)
    selector = (own_table[None, :] == replica_ids).astype(jnp.bfloat16)
    outgoing = jnp.dot(
        selector, prompt_blocks.reshape(prompt_count, -1), preferred_element_type=jnp.float32
    )
    outgoing = outgoing.astype(jnp.bfloat16).reshape(
        node_count, prompt_blocks.shape[1], prompt_blocks.shape[2]
    )
    crossed = from_behind(outgoing, "group", group_count // 2)
    received = lax.all_to_all(crossed, "node", split_axis=0, concat_axis=0, tiled=True)
    slot_queries = new_queries[0, 0]
    own_rows = new_rows[0, 0]
    whole_cache = lax.all_gather(received, "chip", axis=1, tiled=True)
    numerator, row_total = attend(slot_queries, whole_cache, own_rows, slot_lengths)
    context = numerator / row_total[..., None] * is_live.astype(jnp.float32)[:, None, None, None]
    new_context = context.astype(jnp.bfloat16)[None, None]
    standing_num, standing_total = attend(
        resident_queries[0, 0], resident_cache[0, 0], resident_rows[0, 0], resident_lengths[0, 0]
    )
    resident_context = (standing_num / standing_total[..., None]).astype(jnp.bfloat16)[None, None]
    return (new_context, resident_context)


def solution(mesh):
    in_specs = (
        P("group", "node", None, "chip", None),
        P(),
        P(),
        P("group", "node", None, None, "chip", None),
        P("group", "node", None, None, None),
        P("group", "node", None, None, None),
        P("group", "node", None, None, "chip", None),
        P("group", "node", None, None, None),
        P("group", "node", None),
    )
    out_specs = (
        P("group", "node", None, None, "chip", None),
        P("group", "node", None, None, "chip", None),
    )
    return jax.shard_map(
        on_device, mesh=mesh, in_specs=in_specs, out_specs=out_specs, check_vma=False
    )
```

profile of v0, /device:TPU:14, one launch (start us, length us, event | category | flops | bytes accessed | tf_op | source)
XLA Modules:
  0.0 144.5 jit_solution(12564295837071926604)
XLA Ops:
  7.2 1.1 reshape_squeeze.3
  8.3 0.9 dynamic-slice_reduce_fusion
  9.2 0.3 convolution_convert_fusion
  9.5 0.4 reshape.89
  9.9 4.2 %collective-permute-start = (bf16[16,24,576]{2,1,0:T(8,128)(2,1)S(1)}, bf16[16,24,576]{2,1,0:T(8,128)(2,1)S(1)}, u32[]{:S(2)}, u32[]{:S(2)}) collective-permute-start(bf16[16,24,576]{2,1,0:T(8,128)(2,1)S(1)} %reshape.89), channel_id=1, source_target_pairs={{0,512},{128,640},{256,768},{384,896},{512,0},{640,128},{768,256},... | collective-permute-start | bytes 1327112 | tf_op jit(solution)/shard_map/ppermute | solution.py:15
  14.1 22.1 %collective-permute-done = bf16[16,24,576]{2,1,0:T(8,128)(2,1)S(1)} collective-permute-done((bf16[16,24,576]{2,1,0:T(8,128)(2,1)S(1)}, bf16[16,24,576]{2,1,0:T(8,128)(2,1)S(1)}, u32[]{:S(2)}, u32[]{:S(2)}) %collective-permute-start) | collective-permute-done | bytes 442400 | tf_op jit(solution)/shard_map/ppermute | solution.py:15
  36.1 27.0 %all_to_all.5 = bf16[16,24,576]{2,1,0:T(8,128)(2,1)} all-to-all(bf16[16,24,576]{2,1,0:T(8,128)(2,1)S(1)} %collective-permute-done), channel_id=1, replica_groups=mesh['group'=8,'node'=16,'chip'=8] {'node'}, dimensions={0} | all-to-all | bytes 884736 | tf_op jit(solution)/shard_map/all_to_all | solution.py:99
  63.2 0.7 fusion.57
  64.0 5.9 %copy.11 = bf16[1,1,3,1024,576]{4,3,2,1,0:T(8,128)(2,1)} copy(bf16[1,1,3,1024,576]{3,4,2,1,0:T(8,128)(2,1)} %param.14) | data formatting | bytes 7077888 | tf_op args[5]
  69.9 0.1 iota_compare_fusion
  70.0 0.3 fusion.61
  70.3 3.0 %fusion.60 = (f32[3,2,16]{2,1,0:T(2,128)S(1)}, f32[3,2,16,1024]{3,2,1,0:T(8,128)S(1)}) fusion(bf16[1,1,3,1024,576]{3,4,2,1,0:T(8,128)(2,1)} %param.14, bf16[1,1,3,2,16,576]{5,4,3,2,1,0:T(8,128)(2,1)S(1)} %copy-done.3, pred[3,1024]{1,0:T(4,128)(4,1)S(1)} %iota_compare_fusion), kind=kOutput, calls=%fused_computation.64 | convolution fusion | flops 113541024 | bytes 4046208 | tf_op jit(solution)/shard_map/bshc,blc->bshl/dot_general | solution.py:20
  73.4 0.2 fusion.36
  73.6 0.7 select_reduce_fusion
  74.3 0.1 iota_compare_fusion.1
  74.4 0.2 fusion.51
  74.7 1.1 fusion.59
  75.7 1.3 fusion.29
  77.1 54.3 %all-gather.2.cloned.1.call-done = bf16[16,192,576]{2,1,0:T(8,128)(2,1)} async-done(((bf16[16,24,576]{2,1,0:T(8,128)(2,1)}), bf16[16,192,576]{2,1,0:T(8,128)(2,1)}) %all-gather.2.cloned.1.call-update) | async-done | bytes 3538960 | tf_op jit(solution)/shard_map/all_gather | solution.py:102
  131.4 3.9 %fusion.58 = (f32[16,2,16]{2,1,0:T(2,128)S(1)}, f32[16,2,16,192]{3,2,1,0:T(8,128)S(1)}) fusion(bf16[1,1,16,2,16,576]{5,4,3,2,1,0:T(8,128)(2,1)S(1)} %copy-done, bf16[16,192,576]{2,1,0:T(8,128)(2,1)} %all-gather.2.cloned.1.call-done, pred[16,192]{1,0:T(8,128)(4,1)S(1)} %iota_compare_fusion.1), kind=kOutput, calls=%fused_computation.62 | convolution fusion | flops 113540608 | bytes 4527104 | tf_op jit(solution)/shard_map/bshc,blc->bshl/dot_general | solution.py:20
  135.3 0.3 fusion.34
  135.6 0.1 fusion.46
  135.7 0.4 fusion.45
  136.1 1.6 %fusion.25 = bf16[1,1,16,2,16,512]{5,4,3,2,1,0:T(8,128)(2,1)} fusion(f32[16,2,16,512]{3,2,1,0:T(8,128)S(1)} %fusion.45, bf16[16,192,576]{2,1,0:T(8,128)(2,1)S(1)} %copy-done.2, f32[16]{0:T(128)S(1)} %convert_element_type.32, f32[16,2,16]{2,1,0:T(2,128)S(1)} %add.48, f32[16,2,16,192]{3,2,1,0:T(8,128)S(1)} %get-tuple-element.5, f32[16,2,16]{2,1,0:T(2,128)S(1)} %max.14), kind=kOutput, calls=%fused_computation.18 | convolution fusion | flops 101908480 | bytes 5276160 | tf_op jit(solution)/shard_map/bshl,bld->bshd/dot_general | solution.py:38
  (23 shorter events, 0.2 us)
Async XLA Ops:
  7.2 67.5 %copy-start = (bf16[1,1,16,2,16,576]{5,4,3,2,1,0:T(8,128)(2,1)S(1)}, bf16[1,1,16,2,16,576]{5,4,3,2,1,0:T(8,128)(2,1)}, u32[]{:S(2)}) copy-start(bf16[1,1,16,2,16,576]{5,4,3,2,1,0:T(8,128)(2,1)} %param.12) | copy-start | bytes 1769476
  7.2 124.2 %all-gather.2.cloned.1.call-start = ((), (), s32[]{:S(2)}) async-start(), calls=%async_computation.1 | async-start | bytes 4423680 | tf_op jit(solution)/shard_map/all_gather | solution.py:102
  9.9 26.3 %collective-permute-start = (bf16[16,24,576]{2,1,0:T(8,128)(2,1)S(1)}, bf16[16,24,576]{2,1,0:T(8,128)(2,1)S(1)}, u32[]{:S(2)}, u32[]{:S(2)}) collective-permute-start(bf16[16,24,576]{2,1,0:T(8,128)(2,1)S(1)} %reshape.89), channel_id=1, source_target_pairs={{0,512},{128,640},{256,768},{384,896},{512,0},{640,128},{768,256},... | collective-permute-start | bytes 1327112 | tf_op jit(solution)/shard_map/ppermute | solution.py:15
  63.2 6.8 %copy-start.6 = (s32[1,1,3]{2,1,0:T(1,128)S(1)}, s32[1,1,3]{2,1,0:T(1,128)}, u32[]{:S(2)}) copy-start(s32[1,1,3]{2,1,0:T(1,128)} %param.17) | copy-start | bytes 40
  63.2 6.8 %copy-start.3 = (bf16[1,1,3,2,16,576]{5,4,3,2,1,0:T(8,128)(2,1)S(1)}, bf16[1,1,3,2,16,576]{5,4,3,2,1,0:T(8,128)(2,1)}, u32[]{:S(2)}) copy-start(bf16[1,1,3,2,16,576]{5,4,3,2,1,0:T(8,128)(2,1)} %param.15) | copy-start | bytes 331780
  63.2 6.8 %copy-start.5 = (bf16[1,1,3,2,576]{4,3,2,1,0:T(2,128)(2,1)S(1)}, bf16[1,1,3,2,576]{4,3,2,1,0:T(2,128)(2,1)}, u32[]{:S(2)}) copy-start(bf16[1,1,3,2,576]{4,3,2,1,0:T(2,128)(2,1)} %param.16) | copy-start | bytes 20740
  69.9 4.7 %copy-start.4 = (bf16[1,1,16,2,576]{4,3,2,1,0:T(2,128)(2,1)S(1)}, bf16[1,1,16,2,576]{4,3,2,1,0:T(2,128)(2,1)}, u32[]{:S(2)}) copy-start(bf16[1,1,16,2,576]{4,3,2,1,0:T(2,128)(2,1)} %param.13) | copy-start | bytes 110596
  69.9 5.8 %copy-start.1 = (bf16[1,1,3,1024,576]{4,3,2,1,0:T(8,128)(2,1)S(1)}, bf16[1,1,3,1024,576]{4,3,2,1,0:T(8,128)(2,1)}, u32[]{:S(2)}) copy-start(bf16[1,1,3,1024,576]{4,3,2,1,0:T(8,128)(2,1)} %copy.11) | copy-start | bytes 10616836
  131.4 4.7 %copy-start.2 = (bf16[16,192,576]{2,1,0:T(8,128)(2,1)S(1)}, bf16[16,192,576]{2,1,0:T(8,128)(2,1)}, u32[]{:S(2)}) copy-start(bf16[16,192,576]{2,1,0:T(8,128)(2,1)} %all-gather.2.cloned.1.call-done) | copy-start | bytes 10616836
Sparse Core Ops, SparseCore 0:
  63.3 68.0 all-gather.1
where the time goes:
time: 146 us; the launch traced here: 145 us
  waiting for transfers between devices  76.4 us (52%)
  blocking collectives  27 us (18%)
  between operations  14.2 us (10%)
  matrix products  12.1 us (8%)
  local copies, waits for them, and re-layouts  8.31 us (6%)
  starting transfers between devices  4.25 us (3%)
  other arithmetic  2.26 us (2%)
    all_gather x1, waiting for transfers between devices, on_device(): whole_cache = lax.all_gather(received, 'chip', axis=1, tiled=True)  54.3 us
    all_to_all x1, blocking collectives, on_device(): lax.all_to_all(crossed, 'node', split_axis=0, concat_axis=0, tiled=True)  27 us
    ppermute x1, waiting for transfers between devices, from_behind(): return lax.ppermute(value, axis, pairs)  22.1 us
    dot_general x4, matrix products, key_scores(): jnp.einsum('bshc,blc->bshl', queries, keys_block, preferred_element_type=...  8.29 us
    unnamed x15, local copies, waits for them, and re-layouts  5.97 us
    ppermute x1, starting transfers between devices, from_behind(): return lax.ppermute(value, axis, pairs)  4.21 us
    dot_general x2, matrix products, weigh(): jnp.einsum('bshl,bld->bshd', cache_exp.astype(jnp.bfloat16), keys_cache[:...  2.93 us
  transfers between devices with their start and end apart: 2, of which 2 were waited for; matrix products, arithmetic and copies ran while one was open for 10% of the time, Pallas kernels for 0%

commit v1 on v0

v1 whole, which is shorter than its diff:
```python
import functools

import jax
import jax.numpy as jnp
from jax import lax
from jax.experimental import pallas as pl
from jax.experimental.pallas import tpu as pltpu
from jax.sharding import Mesh
from jax.sharding import PartitionSpec as P

LATENT = 512
LANES = 128
score_scale = 1.0 / 192.0**0.5

SMEM = pl.BlockSpec(memory_space=pltpu.SMEM)
VMEM = pl.BlockSpec(memory_space=pltpu.VMEM)


def dot_rows(left, right):
    return lax.dot_general(
        left, right, (((1,), (1,)), ((), ())), preferred_element_type=jnp.float32
    )


def dot_plain(left, right):
    return lax.dot_general(
        left, right, (((1,), (0,)), ((), ())), preferred_element_type=jnp.float32
    )


def pad_rows(rows, count):
    wide = rows.astype(jnp.float32)
    below = jnp.zeros((count - rows.shape[0], rows.shape[1]), jnp.float32)
    return jnp.concatenate([wide, below], axis=0).astype(jnp.bfloat16)


def own_mask(rows, columns, heads, steps):
    step = (lax.broadcasted_iota(jnp.int32, (rows, columns), 0) // heads) % steps
    return lax.broadcasted_iota(jnp.int32, (rows, columns), 1) <= step


def resident_kernel(heads, lengths, queries, keys_t, own, out):
    rows = queries.shape[1]
    for b in range(queries.shape[0]):
        q = queries[b]
        scores = dot_plain(q, keys_t[b]) * score_scale
        position = lax.broadcasted_iota(jnp.int32, (1, scores.shape[1]), 1)
        scores = jnp.where(position < lengths[b], scores, -jnp.inf)
        own_rows = pad_rows(own[b], 8)
        own_scores = dot_rows(q, own_rows) * score_scale
        seen = own_mask(rows, 8, heads, own.shape[1])
        own_scores = jnp.where(seen, own_scores, -jnp.inf)
        top = jnp.maximum(
            jnp.max(scores, axis=1, keepdims=True), jnp.max(own_scores, axis=1, keepdims=True)
        )
        e = jnp.exp(scores - top)
        own_e = jnp.exp(own_scores - top)
        total = jnp.sum(e, axis=1, keepdims=True) + jnp.sum(own_e, axis=1, keepdims=True)
        sums = dot_rows(e.astype(jnp.bfloat16), keys_t[b, :LATENT, :])
        sums = sums + dot_plain(own_e.astype(jnp.bfloat16), own_rows[:, :LATENT])
        out[b] = (sums / total).astype(jnp.bfloat16)


def place_kernel(per, plan, first, second, out):
    prompts = first.shape[0]
    for dest in range(out.shape[0]):
        rotary = []
        for j in range(per):
            pick = plan[dest * per + j]
            at = pick % prompts
            block = jnp.where(pick < prompts, first[at], second[at])
            out[dest, :, j * LATENT : (j + 1) * LATENT] = block[:, :LATENT]
            rotary.append(block[:, LATENT:])
        out[dest, :, per * LATENT :] = jnp.concatenate(rotary, axis=1)


def slot_kernel(per, chunk, heads, steps, plan, queries, kv, own, out, held, sems):
    blocks = queries.shape[0]
    rows = blocks * queries.shape[2]
    rotary = queries.shape[3] - LATENT
    column = lax.broadcasted_iota(jnp.int32, (1, kv.shape[0]), 1)
    came_by = column // chunk
    copies = []
    for j in range(per):
        length = plan[blocks * per + j]
        turn = plan[blocks * per + per + j]
        q = queries[:, j].reshape(rows, queries.shape[3])
        blank = jnp.zeros((rows, rotary), jnp.bfloat16)
        q_rotary = jnp.concatenate([blank] * j + [q[:, LATENT:]] + [blank] * (per - 1 - j), axis=1)
        latents = kv[:, j * LATENT : (j + 1) * LATENT]
        scores = dot_rows(q[:, :LATENT], latents) + dot_rows(q_rotary, kv[:, per * LATENT :])
        source_chip = (turn + blocks - came_by) % blocks
        position = source_chip * chunk + (column - came_by * chunk)
        scores = jnp.where(position < length, scores * score_scale, -jnp.inf)
        own_rows = own[j]
        own_scores = dot_rows(q, own_rows) * score_scale
        own_scores = jnp.where(
            own_mask(rows, own.shape[1], heads, steps), own_scores, -jnp.inf
        )
        top = jnp.maximum(
            jnp.max(scores, axis=1, keepdims=True), jnp.max(own_scores, axis=1, keepdims=True)
        )
        e = jnp.exp(scores - top)
        own_e = jnp.exp(own_scores - top)
        total = jnp.sum(e, axis=1, keepdims=True) + jnp.sum(own_e, axis=1, keepdims=True)
        sums = dot_plain(e.astype(jnp.bfloat16), latents)
        sums = sums + dot_plain(own_e.astype(jnp.bfloat16), own_rows[:, :LATENT])
        context = jnp.where(length > 0, sums / total, 0.0).astype(jnp.bfloat16)
        held[j] = context.reshape(blocks, queries.shape[2], LATENT)
        copies.append(pltpu.make_async_copy(held.at[j], out.at[:, j], sems.at[j]))
        copies[-1].start()
    for copy in copies:
        copy.wait()


def call(kernel, shape, in_specs, *operands, out_specs=VMEM, scratch=()):
    return pl.pallas_call(
        kernel,
        out_shape=jax.ShapeDtypeStruct(shape, jnp.bfloat16),
        in_specs=in_specs,
        out_specs=out_specs,
        scratch_shapes=scratch,
        compiler_params=pltpu.CompilerParams(vmem_limit_bytes=40 * 2**20),
    )(*operands)


def plan_of(sizes, lengths, replica):
    groups, halves, ys, chips = sizes
    per = halves * ys // chips
    source_group = (lax.axis_index("group") + groups // 2) % groups
    half, here, chip = lax.axis_index("xh"), lax.axis_index("y"), lax.axis_index("chip")
    prompts = replica.shape[2]
    start, size = (source_group, chip * per, 0), (1, per, prompts)
    to = lax.dynamic_slice(replica, start, size)
    long = lax.dynamic_slice(lengths, start, size)
    target = half * ys + lax.broadcasted_iota(jnp.int32, (ys, per, prompts), 0)
    turn = (half + lax.broadcasted_iota(jnp.int32, (ys, per, prompts), 1)) % halves
    which = lax.broadcasted_iota(jnp.int32, (ys, per, prompts), 2)
    pick = jnp.sum(jnp.where(to == target, which, 0), axis=2) + turn[:, :, 0] * prompts
    held = jnp.sum(jnp.where(to[0] == half * ys + here, long[0], 0), axis=1)
    slot = chip * per + lax.broadcasted_iota(jnp.int32, (per,), 0)
    return jnp.concatenate([pick.reshape(-1), held, (slot + slot // per) % ys])


def hand_over_pairs(groups, halves, ys, chips, turn):
    per = halves * ys // chips
    pairs = []
    for group in range(groups):
        for half in range(halves):
            for y in range(ys):
                for chip in range(chips):
                    node = half * ys + y
                    to = (
                        (group + groups // 2) % groups,
                        (node + turn) % halves,
                        (node + node // per - chip) % ys,
                        node // per,
                    )
                    pairs.append((
                        ((group * halves + half) * ys + y) * chips + chip,
                        ((to[0] * halves + to[1]) * ys + to[2]) * chips + to[3],
                    ))
    return pairs


def on_device(
    sizes,
    prompt_cache,
    prompt_lengths,
    prompt_replica,
    new_queries,
    new_rows,
    resident_cache,
    resident_queries,
    resident_rows,
    resident_lengths,
):
    groups, halves, ys, chips = sizes
    per = halves * ys // chips
    slots, steps, heads, width = new_queries.shape[2:]
    prompts, chunk = prompt_cache.shape[2:4]
    axes = ("group", "xh", "y", "chip")
    first, second = [
        lax.ppermute(prompt_cache[0, 0], axes, hand_over_pairs(*sizes, turn)) for turn in range(2)
    ]
    queries = lax.all_to_all(new_queries[0, 0], "chip", split_axis=0, concat_axis=0, tiled=True)
    queries = queries.reshape(chips, per, steps * heads, width)
    plan = plan_of(sizes, prompt_lengths, prompt_replica)
    own = lax.dynamic_slice_in_dim(new_rows[0, 0], lax.axis_index("chip") * per, per, 0)
    own = jnp.pad(own, ((0, 0), (0, 8 - steps), (0, 0)))
    queries, plan, own = lax.optimization_barrier((queries, plan, own))

    sequences = resident_queries.shape[2]
    resident = call(
        functools.partial(resident_kernel, heads),
        (sequences, steps * heads, LATENT),
        [SMEM, VMEM, VMEM, VMEM],
        resident_lengths.reshape(sequences),
        resident_queries.reshape(sequences, steps * heads, width),
        jnp.swapaxes(resident_cache[0, 0], 1, 2),
        resident_rows[0, 0],
    )

    outgoing = call(
        functools.partial(place_kernel, per),
        (ys, chunk, per * width),
        [SMEM, VMEM, VMEM],
        plan,
        first,
        second,
    )
    kv = lax.all_to_all(outgoing, "y", split_axis=0, concat_axis=0, tiled=True)
    kv = kv.reshape(ys * chunk, per * width)
    context = call(
        functools.partial(slot_kernel, per, chunk, heads, steps),
        (chips, per, steps * heads, LATENT),
        [SMEM, VMEM, VMEM, VMEM],
        plan,
        queries,
        kv,
        own,
        out_specs=pl.BlockSpec(memory_space=pltpu.MemorySpace.HBM),
        scratch=[
            pltpu.VMEM((per, chips, steps * heads, LATENT), jnp.bfloat16),
            pltpu.SemaphoreType.DMA((per,)),
        ],
    )
    context = context.reshape(1, 1, slots, steps, heads, LATENT)
    new_context = lax.all_to_all(context, "chip", split_axis=2, concat_axis=2, tiled=True)
    resident_context = resident.reshape(1, 1, sequences, steps, heads, LATENT)
    return (new_context, resident_context)


def solution(mesh):
    groups, nodes, chips = mesh.devices.shape
    halves = 2
    sizes = (groups, halves, nodes // halves, chips)
    fine = Mesh(mesh.devices.reshape(sizes), ("group", "xh", "y", "chip"))
    node = ("xh", "y")
    in_specs = (
        P("group", node, None, "chip", None),
        P(),
        P(),
        P("group", node, None, None, "chip", None),
        P("group", node, None, None, None),
        P("group", node, None, None, None),
        P("group", node, None, None, "chip", None),
        P("group", node, None, None, None),
        P("group", node, None),
    )
    out_specs = (
        P("group", node, None, None, "chip", None),
        P("group", node, None, None, "chip", None),
    )
    return jax.shard_map(
        functools.partial(on_device, sizes),
        mesh=fine,
        in_specs=in_specs,
        out_specs=out_specs,
        check_vma=False,
    )
```

time: 146 us -> 99.9 us (0.68)
  waiting for transfers between devices: 76.4 us -> 29.7 us
  starting transfers between devices: 4.25 us -> 36.6 us
  between operations: 14.2 us -> 0.8 us
  matrix products: 12.1 us -> 0 us
  Pallas kernels: 0 us -> 6.6 us
  blocking collectives: 27 us -> 21.5 us
  local copies, waits for them, and re-layouts: 8.31 us -> 4.03 us
  other arithmetic: 2.26 us -> 0.34 us
    all_gather x1 -> x0, waiting for transfers between devices: 54.3 us -> none  [on_device(): whole_cache = lax.all_gather(received, 'chip', axis=1, tiled=True)]
    all_to_all x0 -> x2, waiting for transfers between devices: none -> 29.7 us  [the longest x1 18.5 us: on_device(): lax.all_to_all(new_queries[0, 0], 'chip', split_axis=0, concat_axis=0, ti...]
    ppermute x1 -> x2, starting transfers between devices: 4.21 us -> 29.5 us  [on_device(): lax.ppermute(prompt_cache[0, 0], axes, hand_over_pairs(*sizes, turn))]
    ppermute x1 -> x2, waiting for transfers between devices: 22.1 us -> 0.01 us  [on_device(): lax.ppermute(prompt_cache[0, 0], axes, hand_over_pairs(*sizes, turn))]
    dot_general x9 -> x0, matrix products: 12.1 us -> none  [the longest x4 8.29 us: key_scores(): jnp.einsum('bshc,blc->bshl', queries, keys_block, preferred_element_type=...]
    all_to_all x0 -> x2, starting transfers between devices: none -> 7.06 us  [the longest x1 3.55 us: on_device(): lax.all_to_all(new_queries[0, 0], 'chip', split_axis=0, concat_axis=0, ti...]
    pallas_call x0 -> x3, Pallas kernels: none -> 6.6 us  [call(): pl.pallas_call(kernel, out_shape=jax.ShapeDtypeStruct(shape, jnp.bfloat16...]
    all_to_all x1, blocking collectives: 27 us -> 21.5 us  [on_device(): kv = lax.all_to_all(outgoing, 'y', split_axis=0, concat_axis=0, tiled=True)]
  transfers between devices with their start and end apart: 2 -> 4, of which waited for: 2 -> 2; matrix products, arithmetic and copies ran while one was open for 10% -> 2% of each run, Pallas kernels for 0% -> 3%
where the time goes in v1:
time: 99.9 us; the launch traced here: 99.5 us
  starting transfers between devices  36.6 us (37%)
  waiting for transfers between devices  29.7 us (30%)
  blocking collectives  21.5 us (22%)
  Pallas kernels  6.6 us (7%)
  local copies, waits for them, and re-layouts  4.03 us (4%)
    ppermute x2, starting transfers between devices, on_device(): lax.ppermute(prompt_cache[0, 0], axes, hand_over_pairs(*sizes, turn))  29.5 us
    all_to_all x1, blocking collectives, on_device(): kv = lax.all_to_all(outgoing, 'y', split_axis=0, concat_axis=0, tiled=True)  21.5 us
    all_to_all x1, waiting for transfers between devices, on_device(): lax.all_to_all(new_queries[0, 0], 'chip', split_axis=0, concat_axis=0, ti...  18.5 us
    all_to_all x1, waiting for transfers between devices, on_device(): lax.all_to_all(context, 'chip', split_axis=2, concat_axis=2, tiled=True)  11.1 us
    pallas_call x3, Pallas kernels, call(): pl.pallas_call(kernel, out_shape=jax.ShapeDtypeStruct(shape, jnp.bfloat16...  6.6 us
    all_to_all x1, starting transfers between devices, on_device(): lax.all_to_all(new_queries[0, 0], 'chip', split_axis=0, concat_axis=0, ti...  3.55 us
    all_to_all x1, starting transfers between devices, on_device(): lax.all_to_all(context, 'chip', split_axis=2, concat_axis=2, tiled=True)  3.51 us
    unnamed x11, local copies, waits for them, and re-layouts  2.81 us
  transfers between devices with their start and end apart: 4, of which 2 were waited for; matrix products, arithmetic and copies ran while one was open for 2% of the time, Pallas kernels for 3%

profile of v1, /device:TPU:14, one launch (start us, length us, event | category | flops | bytes accessed | tf_op | source)
XLA Modules:
  0.0 99.5 jit_solution(2991686036961108052)
XLA Ops:
  0.6 0.0 copy-start
  0.7 21.1 %collective-permute-start = (bf16[4,24,576]{2,1,0:T(8,128)(2,1)}, bf16[4,24,576]{2,1,0:T(8,128)(2,1)S(1)}, u32[]{:S(2)}, u32[]{:S(2)}) collective-permute-start(bf16[4,24,576]{2,1,0:T(8,128)(2,1)} %bitcast.33), channel_id=1, source_target_pairs={{0,512},{1,568},{2,560},{3,552},{4,544},{5,536},{6,528},{7,520},{8... | collective-permute-start | bytes 331784 | tf_op jit(solution)/shard_map/ppermute | solution.py:184
  21.8 8.4 %collective-permute-start.1 = (bf16[4,24,576]{2,1,0:T(8,128)(2,1)}, bf16[4,24,576]{2,1,0:T(8,128)(2,1)S(1)}, u32[]{:S(2)}, u32[]{:S(2)}) collective-permute-start(bf16[4,24,576]{2,1,0:T(8,128)(2,1)} %bitcast.34), channel_id=1, source_target_pairs={{0,576},{1,632},{2,624},{3,616},{4,608},{5,600},{6,592},{7,584},{8... | collective-permute-start | bytes 331784 | tf_op jit(solution)/shard_map/ppermute | solution.py:184
  30.2 3.6 %all-to-all-start = ((bf16[16,2,16,576]{3,2,1,0:T(8,128)(2,1)}), bf16[16,2,16,576]{3,2,1,0:T(8,128)(2,1)S(1)}, u32[]{:S(2)}, u32[]{:S(2)}) async-start(bf16[16,2,16,576]{3,2,1,0:T(8,128)(2,1)} %bitcast.30), calls=%async_computation | async-start | bytes 1310720 | tf_op jit(solution)/shard_map/all_to_all | solution.py:186
  33.8 0.8 constant_dynamic-slice_fusion
  34.6 0.1 copy.19
  34.7 0.1 select_reduce_fusion
  34.8 0.1 copy.20
  34.9 0.1 reduce_sum.21
  35.0 0.1 mul.19
  35.1 0.1 copy.21
  35.2 0.1 fusion
  35.3 0.1 pad_add_fusion.plan
  35.4 18.5 %all-to-all-done = bf16[16,2,16,576]{3,2,1,0:T(8,128)(2,1)S(1)} async-done(((bf16[16,2,16,576]{3,2,1,0:T(8,128)(2,1)}), bf16[16,2,16,576]{3,2,1,0:T(8,128)(2,1)S(1)}, u32[]{:S(2)}, u32[]{:S(2)}) %all-to-all-start) | async-done | bytes 589856 | tf_op jit(solution)/shard_map/all_to_all | solution.py:186
  54.0 0.0 collective-permute-done.first
  54.0 0.7 shard_map.104
  54.6 21.5 %all_to_all.15 = bf16[8,24,1152]{2,1,0:T(8,128)(2,1)S(1)} all-to-all(bf16[8,24,1152]{2,1,0:T(8,128)(2,1)S(1)} %shard_map.104), channel_id=1, replica_groups=mesh['group'=8,'xh'=2,'y'=8,'chip'=8] {'y'}, dimensions={0} | all-to-all | bytes 884736 | tf_op jit(solution)/shard_map/all_to_all | solution.py:212
  76.1 2.7 %shard_map.105 = bf16[8,2,32,512]{3,2,1,0:T(8,128)(2,1)} custom-call(s32[20]{0:T(128)S(1)} %pad_add_fusion.plan, bf16[8,2,32,576]{3,2,1,0:T(8,128)(2,1)S(1)} %bitcast.24, bf16[192,1152]{1,0:T(8,128)(2,1)S(1)} %bitcast.25, bf16[2,8,576]{2,1,0:T(8,128)(2,1)S(1)} %pad.4.own), custom_call_target="tpu_custom_call" | custom-call | tf_op jit(solution)/shard_map/pallas_call | solution.py:117
  78.8 3.5 %all-to-all-start.2 = ((bf16[1,1,16,2,16,512]{5,4,3,1,0,2:T(8,128)(2,1)}), bf16[1,1,16,2,16,512]{5,4,3,1,0,2:T(8,128)(2,1)S(1)}, u32[]{:S(2)}, u32[]{:S(2)}) async-start(bf16[1,1,16,2,16,512]{5,4,3,1,0,2:T(8,128)(2,1)} %bitcast.8), calls=%async_computation.2 | async-start | bytes 1048576 | tf_op jit(solution)/shard_map/all_to_all | solution.py:229
  82.3 0.0 copy-start.1
  82.3 2.0 %copy-done.1 = bf16[1,1,3,1024,576]{3,4,2,1,0:T(8,128)(2,1)S(1)} copy-done((bf16[1,1,3,1024,576]{3,4,2,1,0:T(8,128)(2,1)S(1)}, bf16[1,1,3,1024,576]{3,4,2,1,0:T(8,128)(2,1)}, u32[]{:S(2)}) %copy-start.1) | copy-done | bytes 3538968
  84.3 3.2 %shard_map.106 = bf16[3,32,512]{2,1,0:T(8,128)(2,1)} custom-call(s32[3]{0:T(128)S(1)} %bitcast.28, bf16[3,32,576]{2,1,0:T(8,128)(2,1)S(1)} %bitcast.26, bf16[3,576,1024]{2,1,0:T(8,128)(2,1)S(1)} %bitcast.23, bf16[3,2,576]{2,1,0:T(2,128)(2,1)S(1)} %bitcast.27), custom_call_target="tpu_custom_call" | custom-call | tf_op jit(solution)/shard_map/pallas_call | solution.py:117
  87.6 11.1 %all-to-all-done.2 = bf16[1,1,16,2,16,512]{5,4,3,1,0,2:T(8,128)(2,1)S(1)} async-done(((bf16[1,1,16,2,16,512]{5,4,3,1,0,2:T(8,128)(2,1)}), bf16[1,1,16,2,16,512]{5,4,3,1,0,2:T(8,128)(2,1)S(1)}, u32[]{:S(2)}, u32[]{:S(2)}) %all-to-all-start.2) | async-done | bytes 524320 | tf_op jit(solution)/shard_map/all_to_all | solution.py:229
  98.7 0.8 copy.25
  (16 shorter events, 0.1 us)
Async XLA Ops:
  0.6 34.5 %copy-start = (bf16[1,1,16,2,576]{4,3,2,1,0:T(2,128)(2,1)S(1)}, bf16[1,1,16,2,576]{4,3,2,1,0:T(2,128)(2,1)}, u32[]{:S(2)}) copy-start(bf16[1,1,16,2,576]{4,3,2,1,0:T(2,128)(2,1)} %param.13) | copy-start | bytes 110596
  0.6 81.7 %copy-start.4 = (s32[1,1,3]{2,1,0:T(1,128)S(1)}, s32[1,1,3]{2,1,0:T(1,128)}, u32[]{:S(2)}) copy-start(s32[1,1,3]{2,1,0:T(1,128)} %param.17) | copy-start | bytes 40
  0.7 81.7 %copy-start.2 = (bf16[1,1,3,2,16,576]{5,4,3,2,1,0:T(8,128)(2,1)S(1)}, bf16[1,1,3,2,16,576]{5,4,3,2,1,0:T(8,128)(2,1)}, u32[]{:S(2)}) copy-start(bf16[1,1,3,2,16,576]{5,4,3,2,1,0:T(8,128)(2,1)} %param.15) | copy-start | bytes 331780
  0.7 81.7 %copy-start.3 = (bf16[1,1,3,2,576]{4,3,2,1,0:T(2,128)(2,1)S(1)}, bf16[1,1,3,2,576]{4,3,2,1,0:T(2,128)(2,1)}, u32[]{:S(2)}) copy-start(bf16[1,1,3,2,576]{4,3,2,1,0:T(2,128)(2,1)} %param.16) | copy-start | bytes 20740
  0.7 53.3 %collective-permute-start = (bf16[4,24,576]{2,1,0:T(8,128)(2,1)}, bf16[4,24,576]{2,1,0:T(8,128)(2,1)S(1)}, u32[]{:S(2)}, u32[]{:S(2)}) collective-permute-start(bf16[4,24,576]{2,1,0:T(8,128)(2,1)} %bitcast.33), channel_id=1, source_target_pairs={{0,512},{1,568},{2,560},{3,552},{4,544},{5,536},{6,528},{7,520},{8... | collective-permute-start | bytes 331784 | tf_op jit(solution)/shard_map/ppermute | solution.py:184
  21.8 32.2 %collective-permute-start.1 = (bf16[4,24,576]{2,1,0:T(8,128)(2,1)}, bf16[4,24,576]{2,1,0:T(8,128)(2,1)S(1)}, u32[]{:S(2)}, u32[]{:S(2)}) collective-permute-start(bf16[4,24,576]{2,1,0:T(8,128)(2,1)} %bitcast.34), channel_id=1, source_target_pairs={{0,576},{1,632},{2,624},{3,616},{4,608},{5,600},{6,592},{7,584},{8... | collective-permute-start | bytes 331784 | tf_op jit(solution)/shard_map/ppermute | solution.py:184
  30.2 23.7 %all-to-all-start = ((bf16[16,2,16,576]{3,2,1,0:T(8,128)(2,1)}), bf16[16,2,16,576]{3,2,1,0:T(8,128)(2,1)S(1)}, u32[]{:S(2)}, u32[]{:S(2)}) async-start(bf16[16,2,16,576]{3,2,1,0:T(8,128)(2,1)} %bitcast.30), calls=%async_computation | async-start | bytes 1310720 | tf_op jit(solution)/shard_map/all_to_all | solution.py:186
  78.8 19.9 %all-to-all-start.2 = ((bf16[1,1,16,2,16,512]{5,4,3,1,0,2:T(8,128)(2,1)}), bf16[1,1,16,2,16,512]{5,4,3,1,0,2:T(8,128)(2,1)S(1)}, u32[]{:S(2)}, u32[]{:S(2)}) async-start(bf16[1,1,16,2,16,512]{5,4,3,1,0,2:T(8,128)(2,1)} %bitcast.8), calls=%async_computation.2 | async-start | bytes 1048576 | tf_op jit(solution)/shard_map/all_to_all | solution.py:229
  82.3 2.0 %copy-start.1 = (bf16[1,1,3,1024,576]{3,4,2,1,0:T(8,128)(2,1)S(1)}, bf16[1,1,3,1024,576]{3,4,2,1,0:T(8,128)(2,1)}, u32[]{:S(2)}) copy-start(bf16[1,1,3,1024,576]{3,4,2,1,0:T(8,128)(2,1)} %param.14) | copy-start | bytes 10616836

commit v2 on v1

--- a/solution.py
+++ b/solution.py
@@ -180,15 +180,16 @@
     slots, steps, heads, width = new_queries.shape[2:]
     prompts, chunk = prompt_cache.shape[2:4]
     axes = ("group", "xh", "y", "chip")
+    plan = plan_of(sizes, prompt_lengths, prompt_replica)
+    own = lax.dynamic_slice_in_dim(new_rows[0, 0], lax.axis_index("chip") * per, per, 0)
+    own = jnp.pad(own, ((0, 0), (0, 8 - steps), (0, 0)))
+    plan, own, prompt_cache = lax.optimization_barrier((plan, own, prompt_cache))
     first, second = [
         lax.ppermute(prompt_cache[0, 0], axes, hand_over_pairs(*sizes, turn)) for turn in range(2)
     ]
     queries = lax.all_to_all(new_queries[0, 0], "chip", split_axis=0, concat_axis=0, tiled=True)
     queries = queries.reshape(chips, per, steps * heads, width)
-    plan = plan_of(sizes, prompt_lengths, prompt_replica)
-    own = lax.dynamic_slice_in_dim(new_rows[0, 0], lax.axis_index("chip") * per, per, 0)
-    own = jnp.pad(own, ((0, 0), (0, 8 - steps), (0, 0)))
-    queries, plan, own = lax.optimization_barrier((queries, plan, own))
+    queries, plan = lax.optimization_barrier((queries, plan))
 
     sequences = resident_queries.shape[2]
     resident = call(

time: 99.9 us -> 94.6 us (0.947); the launches traced: 99.5 us -> 93 us
  waiting for transfers between devices: 29.7 us -> 14.6 us
  blocking collectives: 21.5 us -> 26.5 us
  starting transfers between devices: 36.6 us -> 40.3 us
    all_to_all x1, waiting for transfers between devices: 18.5 us -> 0.15 us  [on_device(): lax.all_to_all(new_queries[0, 0], 'chip', split_axis=0, concat_axis=0, ti...]
    all_to_all x1, starting transfers between devices: 3.55 us -> 16.8 us  [on_device(): lax.all_to_all(new_queries[0, 0], 'chip', split_axis=0, concat_axis=0, ti...]
    ppermute x2, starting transfers between devices: 29.5 us -> 19.1 us  [on_device(): lax.ppermute(prompt_cache[0, 0], axes, hand_over_pairs(*sizes, turn))]
    all_to_all x1, blocking collectives: 21.5 us -> 26.5 us  [on_device(): kv = lax.all_to_all(outgoing, 'y', split_axis=0, concat_axis=0, tiled=True)]
    ppermute x2, waiting for transfers between devices: 0.01 us -> 4.16 us  [on_device(): lax.ppermute(prompt_cache[0, 0], axes, hand_over_pairs(*sizes, turn))]
  transfers between devices with their start and end apart: 4 -> 4, of which waited for: 2 -> 3; matrix products, arithmetic and copies ran while one was open for 2% -> 2% of each run, Pallas kernels for 3% -> 3%
where the time goes in v2:
time: 94.6 us; the launch traced here: 93 us
  starting transfers between devices  40.3 us (43%)
  blocking collectives  26.5 us (28%)
  waiting for transfers between devices  14.6 us (15%)
  Pallas kernels  6.59 us (7%)
  local copies, waits for them, and re-layouts  4.03 us (4%)
    all_to_all x1, blocking collectives, on_device(): kv = lax.all_to_all(outgoing, 'y', split_axis=0, concat_axis=0, tiled=True)  26.5 us
    ppermute x2, starting transfers between devices, on_device(): lax.ppermute(prompt_cache[0, 0], axes, hand_over_pairs(*sizes, turn))  19.1 us
    all_to_all x1, starting transfers between devices, on_device(): lax.all_to_all(new_queries[0, 0], 'chip', split_axis=0, concat_axis=0, ti...  16.8 us
    all_to_all x1, waiting for transfers between devices, on_device(): lax.all_to_all(context, 'chip', split_axis=2, concat_axis=2, tiled=True)  10.3 us
    pallas_call x3, Pallas kernels, call(): pl.pallas_call(kernel, out_shape=jax.ShapeDtypeStruct(shape, jnp.bfloat16...  6.59 us
    all_to_all x1, starting transfers between devices, on_device(): lax.all_to_all(context, 'chip', split_axis=2, concat_axis=2, tiled=True)  4.36 us
    ppermute x2, waiting for transfers between devices, on_device(): lax.ppermute(prompt_cache[0, 0], axes, hand_over_pairs(*sizes, turn))  4.16 us
    unnamed x11, local copies, waits for them, and re-layouts  2.81 us
  transfers between devices with their start and end apart: 4, of which 3 were waited for; matrix products, arithmetic and copies ran while one was open for 2% of the time, Pallas kernels for 3%

profile of v2, /device:TPU:14, one launch (start us, length us, event | category | flops | bytes accessed | tf_op | source)
XLA Modules:
  0.0 93.0 jit_solution(2487435656679868049)
XLA Ops:
  0.6 0.0 copy-start
  0.7 16.8 %all-to-all-start = ((bf16[16,2,16,576]{3,2,1,0:T(8,128)(2,1)}), bf16[16,2,16,576]{3,2,1,0:T(8,128)(2,1)S(1)}, u32[]{:S(2)}, u32[]{:S(2)}) async-start(bf16[16,2,16,576]{3,2,1,0:T(8,128)(2,1)} %bitcast.30), calls=%async_computation | async-start | bytes 1310720 | tf_op jit(solution)/shard_map/all_to_all | solution.py:190
  17.5 0.8 constant_dynamic-slice_fusion
  18.3 0.1 copy.19
  18.4 0.1 select_reduce_fusion
  18.5 0.1 copy.20
  18.5 0.1 reduce_sum.21
  18.7 0.1 mul.19
  18.8 0.1 copy.21
  18.9 0.1 fusion
  19.0 0.1 pad_add_fusion.plan
  19.1 14.3 %collective-permute-start = (bf16[4,24,576]{2,1,0:T(8,128)(2,1)}, bf16[4,24,576]{2,1,0:T(8,128)(2,1)S(1)}, u32[]{:S(2)}, u32[]{:S(2)}) collective-permute-start(bf16[4,24,576]{2,1,0:T(8,128)(2,1)} %bitcast.33), channel_id=1, source_target_pairs={{0,512},{1,568},{2,560},{3,552},{4,544},{5,536},{6,528},{7,520},{8... | collective-permute-start | bytes 331784 | tf_op jit(solution)/shard_map/ppermute | solution.py:188
  33.4 4.8 %collective-permute-start.1 = (bf16[4,24,576]{2,1,0:T(8,128)(2,1)}, bf16[4,24,576]{2,1,0:T(8,128)(2,1)S(1)}, u32[]{:S(2)}, u32[]{:S(2)}) collective-permute-start(bf16[4,24,576]{2,1,0:T(8,128)(2,1)} %bitcast.34), channel_id=1, source_target_pairs={{0,576},{1,632},{2,624},{3,616},{4,608},{5,600},{6,592},{7,584},{8... | collective-permute-start | bytes 331784 | tf_op jit(solution)/shard_map/ppermute | solution.py:188
  38.2 0.1 all-to-all-done
  38.3 4.2 %collective-permute-done.1.second = bf16[4,24,576]{2,1,0:T(8,128)(2,1)S(1)} collective-permute-done((bf16[4,24,576]{2,1,0:T(8,128)(2,1)}, bf16[4,24,576]{2,1,0:T(8,128)(2,1)S(1)}, u32[]{:S(2)}, u32[]{:S(2)}) %collective-permute-start.1) | collective-permute-done | bytes 110624 | tf_op jit(solution)/shard_map/ppermute | solution.py:188
  42.5 0.7 shard_map.104
  43.1 26.5 %all_to_all.15 = bf16[8,24,1152]{2,1,0:T(8,128)(2,1)S(1)} all-to-all(bf16[8,24,1152]{2,1,0:T(8,128)(2,1)S(1)} %shard_map.104), channel_id=1, replica_groups=mesh['group'=8,'xh'=2,'y'=8,'chip'=8] {'y'}, dimensions={0} | all-to-all | bytes 884736 | tf_op jit(solution)/shard_map/all_to_all | solution.py:213
  69.6 2.7 %shard_map.105 = bf16[8,2,32,512]{3,2,1,0:T(8,128)(2,1)} custom-call(s32[20]{0:T(128)S(1)} %pad_add_fusion.plan, bf16[8,2,32,576]{3,2,1,0:T(8,128)(2,1)S(1)} %bitcast.24, bf16[192,1152]{1,0:T(8,128)(2,1)S(1)} %bitcast.25, bf16[2,8,576]{2,1,0:T(8,128)(2,1)S(1)} %pad.4.own), custom_call_target="tpu_custom_call" | custom-call | tf_op jit(solution)/shard_map/pallas_call | solution.py:117
  72.3 4.4 %all-to-all-start.2 = ((bf16[1,1,16,2,16,512]{5,4,3,1,0,2:T(8,128)(2,1)}), bf16[1,1,16,2,16,512]{5,4,3,1,0,2:T(8,128)(2,1)S(1)}, u32[]{:S(2)}, u32[]{:S(2)}) async-start(bf16[1,1,16,2,16,512]{5,4,3,1,0,2:T(8,128)(2,1)} %bitcast.8), calls=%async_computation.2 | async-start | bytes 1048576 | tf_op jit(solution)/shard_map/all_to_all | solution.py:230
  76.7 0.0 copy-start.1
  76.7 2.0 %copy-done.1 = bf16[1,1,3,1024,576]{3,4,2,1,0:T(8,128)(2,1)S(1)} copy-done((bf16[1,1,3,1024,576]{3,4,2,1,0:T(8,128)(2,1)S(1)}, bf16[1,1,3,1024,576]{3,4,2,1,0:T(8,128)(2,1)}, u32[]{:S(2)}) %copy-start.1) | copy-done | bytes 3538968
  78.7 3.2 %shard_map.106 = bf16[3,32,512]{2,1,0:T(8,128)(2,1)} custom-call(s32[3]{0:T(128)S(1)} %bitcast.28, bf16[3,32,576]{2,1,0:T(8,128)(2,1)S(1)} %bitcast.26, bf16[3,576,1024]{2,1,0:T(8,128)(2,1)S(1)} %bitcast.23, bf16[3,2,576]{2,1,0:T(2,128)(2,1)S(1)} %bitcast.27), custom_call_target="tpu_custom_call" | custom-call | tf_op jit(solution)/shard_map/pallas_call | solution.py:117
  82.0 10.3 %all-to-all-done.2 = bf16[1,1,16,2,16,512]{5,4,3,1,0,2:T(8,128)(2,1)S(1)} async-done(((bf16[1,1,16,2,16,512]{5,4,3,1,0,2:T(8,128)(2,1)}), bf16[1,1,16,2,16,512]{5,4,3,1,0,2:T(8,128)(2,1)S(1)}, u32[]{:S(2)}, u32[]{:S(2)}) %all-to-all-start.2) | async-done | bytes 524320 | tf_op jit(solution)/shard_map/all_to_all | solution.py:230
  92.2 0.8 copy.25
  (16 shorter events, 0.1 us)
Async XLA Ops:
  0.6 18.2 %copy-start = (bf16[1,1,16,2,576]{4,3,2,1,0:T(2,128)(2,1)S(1)}, bf16[1,1,16,2,576]{4,3,2,1,0:T(2,128)(2,1)}, u32[]{:S(2)}) copy-start(bf16[1,1,16,2,576]{4,3,2,1,0:T(2,128)(2,1)} %param.13) | copy-start | bytes 110596
  0.6 76.1 %copy-start.4 = (s32[1,1,3]{2,1,0:T(1,128)S(1)}, s32[1,1,3]{2,1,0:T(1,128)}, u32[]{:S(2)}) copy-start(s32[1,1,3]{2,1,0:T(1,128)} %param.17) | copy-start | bytes 40
  0.7 76.1 %copy-start.2 = (bf16[1,1,3,2,16,576]{5,4,3,2,1,0:T(8,128)(2,1)S(1)}, bf16[1,1,3,2,16,576]{5,4,3,2,1,0:T(8,128)(2,1)}, u32[]{:S(2)}) copy-start(bf16[1,1,3,2,16,576]{5,4,3,2,1,0:T(8,128)(2,1)} %param.15) | copy-start | bytes 331780
  0.7 76.1 %copy-start.3 = (bf16[1,1,3,2,576]{4,3,2,1,0:T(2,128)(2,1)S(1)}, bf16[1,1,3,2,576]{4,3,2,1,0:T(2,128)(2,1)}, u32[]{:S(2)}) copy-start(bf16[1,1,3,2,576]{4,3,2,1,0:T(2,128)(2,1)} %param.16) | copy-start | bytes 20740
  0.7 37.6 %all-to-all-start = ((bf16[16,2,16,576]{3,2,1,0:T(8,128)(2,1)}), bf16[16,2,16,576]{3,2,1,0:T(8,128)(2,1)S(1)}, u32[]{:S(2)}, u32[]{:S(2)}) async-start(bf16[16,2,16,576]{3,2,1,0:T(8,128)(2,1)} %bitcast.30), calls=%async_computation | async-start | bytes 1310720 | tf_op jit(solution)/shard_map/all_to_all | solution.py:190
  19.1 19.2 %collective-permute-start = (bf16[4,24,576]{2,1,0:T(8,128)(2,1)}, bf16[4,24,576]{2,1,0:T(8,128)(2,1)S(1)}, u32[]{:S(2)}, u32[]{:S(2)}) collective-permute-start(bf16[4,24,576]{2,1,0:T(8,128)(2,1)} %bitcast.33), channel_id=1, source_target_pairs={{0,512},{1,568},{2,560},{3,552},{4,544},{5,536},{6,528},{7,520},{8... | collective-permute-start | bytes 331784 | tf_op jit(solution)/shard_map/ppermute | solution.py:188
  33.4 9.1 %collective-permute-start.1 = (bf16[4,24,576]{2,1,0:T(8,128)(2,1)}, bf16[4,24,576]{2,1,0:T(8,128)(2,1)S(1)}, u32[]{:S(2)}, u32[]{:S(2)}) collective-permute-start(bf16[4,24,576]{2,1,0:T(8,128)(2,1)} %bitcast.34), channel_id=1, source_target_pairs={{0,576},{1,632},{2,624},{3,616},{4,608},{5,600},{6,592},{7,584},{8... | collective-permute-start | bytes 331784 | tf_op jit(solution)/shard_map/ppermute | solution.py:188
  72.3 19.9 %all-to-all-start.2 = ((bf16[1,1,16,2,16,512]{5,4,3,1,0,2:T(8,128)(2,1)}), bf16[1,1,16,2,16,512]{5,4,3,1,0,2:T(8,128)(2,1)S(1)}, u32[]{:S(2)}, u32[]{:S(2)}) async-start(bf16[1,1,16,2,16,512]{5,4,3,1,0,2:T(8,128)(2,1)} %bitcast.8), calls=%async_computation.2 | async-start | bytes 1048576 | tf_op jit(solution)/shard_map/all_to_all | solution.py:230
  76.7 2.0 %copy-start.1 = (bf16[1,1,3,1024,576]{3,4,2,1,0:T(8,128)(2,1)S(1)}, bf16[1,1,3,1024,576]{3,4,2,1,0:T(8,128)(2,1)}, u32[]{:S(2)}) copy-start(bf16[1,1,3,1024,576]{3,4,2,1,0:T(8,128)(2,1)} %param.14) | copy-start | bytes 10616836

commit v3 on v2

--- a/solution.py
+++ b/solution.py
@@ -58,7 +58,7 @@
         total = jnp.sum(e, axis=1, keepdims=True) + jnp.sum(own_e, axis=1, keepdims=True)
         sums = dot_rows(e.astype(jnp.bfloat16), keys_t[b, :LATENT, :])
         sums = sums + dot_plain(own_e.astype(jnp.bfloat16), own_rows[:, :LATENT])
-        out[b] = (sums / total).astype(jnp.bfloat16)
+        out[b] = (sums * (1.0 / total)).astype(jnp.bfloat16)
 
 
 def place_kernel(per, plan, first, second, out):
@@ -78,8 +78,13 @@
     blocks = queries.shape[0]
     rows = blocks * queries.shape[2]
     rotary = queries.shape[3] - LATENT
-    column = lax.broadcasted_iota(jnp.int32, (1, kv.shape[0]), 1)
+    cached = kv.shape[0]
+    count = cached + own.shape[1]
+    column = lax.broadcasted_iota(jnp.int32, (1, count), 1)
     came_by = column // chunk
+    step = (lax.broadcasted_iota(jnp.int32, (rows, 1), 0) // heads) % steps
+    own_rotary = jnp.concatenate([own[j, :, LATENT:] for j in range(per)], axis=1)
+    key_rotary = jnp.concatenate([kv[:, per * LATENT :], own_rotary], axis=0)
     copies = []
     for j in range(per):
         length = plan[blocks * per + j]
@@ -87,26 +92,21 @@
         q = queries[:, j].reshape(rows, queries.shape[3])
         blank = jnp.zeros((rows, rotary), jnp.bfloat16)
         q_rotary = jnp.concatenate([blank] * j + [q[:, LATENT:]] + [blank] * (per - 1 - j), axis=1)
-        latents = kv[:, j * LATENT : (j + 1) * LATENT]
-        scores = dot_rows(q[:, :LATENT], latents) + dot_rows(q_rotary, kv[:, per * LATENT :])
+        latents = jnp.concatenate(
+            [kv[:, j * LATENT : (j + 1) * LATENT], own[j, :, :LATENT]], axis=0
+        )
+        scores = dot_rows(q[:, :LATENT], latents) + dot_rows(q_rotary, key_rotary)
         source_chip = (turn + blocks - came_by) % blocks
         position = source_chip * chunk + (column - came_by * chunk)
-        scores = jnp.where(position < length, scores * score_scale, -jnp.inf)
-        own_rows = own[j]
-        own_scores = dot_rows(q, own_rows) * score_scale
-        own_scores = jnp.where(
-            own_mask(rows, own.shape[1], heads, steps), own_scores, -jnp.inf
-        )
-        top = jnp.maximum(
-            jnp.max(scores, axis=1, keepdims=True), jnp.max(own_scores, axis=1, keepdims=True)
-        )
+        position = jnp.where(column < cached, position, column - cached)
+        bound = jnp.where(column < cached, length, step + 1)
+        scores = jnp.where(position < bound, scores * score_scale, -jnp.inf)
+        top = jnp.max(scores, axis=1, keepdims=True)
         e = jnp.exp(scores - top)
-        own_e = jnp.exp(own_scores - top)
-        total = jnp.sum(e, axis=1, keepdims=True) + jnp.sum(own_e, axis=1, keepdims=True)
+        total = jnp.sum(e, axis=1, keepdims=True)
         sums = dot_plain(e.astype(jnp.bfloat16), latents)
-        sums = sums + dot_plain(own_e.astype(jnp.bfloat16), own_rows[:, :LATENT])
-        context = jnp.where(length > 0, sums / total, 0.0).astype(jnp.bfloat16)
-        held[j] = context.reshape(blocks, queries.shape[2], LATENT)
+        share = jnp.where(length > 0, 1.0 / total, 0.0)
+        held[j] = (sums * share).astype(jnp.bfloat16).reshape(blocks, queries.shape[2], LATENT)
         copies.append(pltpu.make_async_copy(held.at[j], out.at[:, j], sems.at[j]))
         copies[-1].start()
     for copy in copies:
@@ -139,7 +139,7 @@
     pick = jnp.sum(jnp.where(to == target, which, 0), axis=2) + turn[:, :, 0] * prompts
     held = jnp.sum(jnp.where(to[0] == half * ys + here, long[0], 0), axis=1)
     slot = chip * per + lax.broadcasted_iota(jnp.int32, (per,), 0)
-    return jnp.concatenate([pick.reshape(-1), held, (slot + slot // per) % ys])
+    return jnp.concatenate([pick.reshape(-1), held, (slot + slot // per + 4) % ys])
 
 
 def hand_over_pairs(groups, halves, ys, chips, turn):
@@ -153,7 +153,7 @@
                     to = (
                         (group + groups // 2) % groups,
                         (node + turn) % halves,
-                        (node + node // per - chip) % ys,
+                        (node + node // per + 4 - chip) % ys,
                         node // per,
                     )
                     pairs.append((
@@ -182,7 +182,7 @@
     axes = ("group", "xh", "y", "chip")
     plan = plan_of(sizes, prompt_lengths, prompt_replica)
     own = lax.dynamic_slice_in_dim(new_rows[0, 0], lax.axis_index("chip") * per, per, 0)
-    own = jnp.pad(own, ((0, 0), (0, 8 - steps), (0, 0)))
+    own = jnp.pad(own, ((0, 0), (0, 16 - steps), (0, 0)))
     plan, own, prompt_cache = lax.optimization_barrier((plan, own, prompt_cache))
     first, second = [
         lax.ppermute(prompt_cache[0, 0], axes, hand_over_pairs(*sizes, turn)) for turn in range(2)

time: 94.6 us -> 90.5 us (0.957)
  blocking collectives: 26.5 us -> 20.7 us
  waiting for transfers between devices: 14.6 us -> 17.9 us
    all_to_all x1, waiting for transfers between devices: 0.15 us -> 7.67 us  [on_device(): lax.all_to_all(new_queries[0, 0], 'chip', split_axis=0, concat_axis=0, ti...]
    all_to_all x1, blocking collectives: 26.5 us -> 20.7 us  [on_device(): kv = lax.all_to_all(outgoing, 'y', split_axis=0, concat_axis=0, tiled=True)]
    ppermute x2, waiting for transfers between devices: 4.16 us -> 0.01 us  [on_device(): lax.ppermute(prompt_cache[0, 0], axes, hand_over_pairs(*sizes, turn))]
  transfers between devices with their start and end apart: 4 -> 4, of which waited for: 3 -> 2; matrix products, arithmetic and copies ran while one was open for 2% -> 2% of each run, Pallas kernels for 3% -> 4%
where the time goes in v3:
time: 90.5 us; the launch traced here: 89.4 us
  starting transfers between devices  39.5 us (44%)
  blocking collectives  20.7 us (23%)
  waiting for transfers between devices  17.9 us (20%)
  Pallas kernels  6.29 us (7%)
  local copies, waits for them, and re-layouts  4.03 us (4%)
    all_to_all x1, blocking collectives, on_device(): kv = lax.all_to_all(outgoing, 'y', split_axis=0, concat_axis=0, tiled=True)  20.7 us
    ppermute x2, starting transfers between devices, on_device(): lax.ppermute(prompt_cache[0, 0], axes, hand_over_pairs(*sizes, turn))  18.6 us
    all_to_all x1, starting transfers between devices, on_device(): lax.all_to_all(new_queries[0, 0], 'chip', split_axis=0, concat_axis=0, ti...  16.8 us
    all_to_all x1, waiting for transfers between devices, on_device(): lax.all_to_all(context, 'chip', split_axis=2, concat_axis=2, tiled=True)  10.2 us
    all_to_all x1, waiting for transfers between devices, on_device(): lax.all_to_all(new_queries[0, 0], 'chip', split_axis=0, concat_axis=0, ti...  7.67 us
    pallas_call x3, Pallas kernels, call(): pl.pallas_call(kernel, out_shape=jax.ShapeDtypeStruct(shape, jnp.bfloat16...  6.29 us
    all_to_all x1, starting transfers between devices, on_device(): lax.all_to_all(context, 'chip', split_axis=2, concat_axis=2, tiled=True)  4.03 us
    unnamed x11, local copies, waits for them, and re-layouts  2.81 us
  transfers between devices with their start and end apart: 4, of which 2 were waited for; matrix products, arithmetic and copies ran while one was open for 2% of the time, Pallas kernels for 4%

profile of v3, /device:TPU:14, one launch (start us, length us, event | category | flops | bytes accessed | tf_op | source)
XLA Modules:
  0.0 89.4 jit_solution(14593170383000141838)
XLA Ops:
  0.6 0.0 copy-start
  0.7 16.8 %all-to-all-start = ((bf16[16,2,16,576]{3,2,1,0:T(8,128)(2,1)}), bf16[16,2,16,576]{3,2,1,0:T(8,128)(2,1)S(1)}, u32[]{:S(2)}, u32[]{:S(2)}) async-start(bf16[16,2,16,576]{3,2,1,0:T(8,128)(2,1)} %bitcast.30), calls=%async_computation | async-start | bytes 1310720 | tf_op jit(solution)/shard_map/all_to_all | solution.py:190
  17.5 0.8 constant_dynamic-slice_fusion
  18.3 0.1 copy.19
  18.4 0.1 select_reduce_fusion
  18.5 0.1 copy.20
  18.5 0.1 reduce_sum.21
  18.7 0.1 mul.19
  18.8 0.1 copy.21
  18.9 0.1 fusion
  19.0 0.1 pad_add_fusion.plan
  19.1 8.6 %collective-permute-start = (bf16[4,24,576]{2,1,0:T(8,128)(2,1)}, bf16[4,24,576]{2,1,0:T(8,128)(2,1)S(1)}, u32[]{:S(2)}, u32[]{:S(2)}) collective-permute-start(bf16[4,24,576]{2,1,0:T(8,128)(2,1)} %bitcast.33), channel_id=1, source_target_pairs={{0,544},{1,536},{2,528},{3,520},{4,512},{5,568},{6,560},{7,552},{8... | collective-permute-start | bytes 331784 | tf_op jit(solution)/shard_map/ppermute | solution.py:188
  27.7 10.0 %collective-permute-start.1 = (bf16[4,24,576]{2,1,0:T(8,128)(2,1)}, bf16[4,24,576]{2,1,0:T(8,128)(2,1)S(1)}, u32[]{:S(2)}, u32[]{:S(2)}) collective-permute-start(bf16[4,24,576]{2,1,0:T(8,128)(2,1)} %bitcast.34), channel_id=1, source_target_pairs={{0,608},{1,600},{2,592},{3,584},{4,576},{5,632},{6,624},{7,616},{8... | collective-permute-start | bytes 331784 | tf_op jit(solution)/shard_map/ppermute | solution.py:188
  37.7 7.7 %all-to-all-done = bf16[16,2,16,576]{3,2,1,0:T(8,128)(2,1)S(1)} async-done(((bf16[16,2,16,576]{3,2,1,0:T(8,128)(2,1)}), bf16[16,2,16,576]{3,2,1,0:T(8,128)(2,1)S(1)}, u32[]{:S(2)}, u32[]{:S(2)}) %all-to-all-start) | async-done | bytes 589856 | tf_op jit(solution)/shard_map/all_to_all | solution.py:190
  45.4 0.0 collective-permute-done.first
  45.4 0.7 shard_map.104
  46.0 20.7 %all_to_all.15 = bf16[8,24,1152]{2,1,0:T(8,128)(2,1)S(1)} all-to-all(bf16[8,24,1152]{2,1,0:T(8,128)(2,1)S(1)} %shard_map.104), channel_id=1, replica_groups=mesh['group'=8,'xh'=2,'y'=8,'chip'=8] {'y'}, dimensions={0} | all-to-all | bytes 884736 | tf_op jit(solution)/shard_map/all_to_all | solution.py:213
  66.7 2.4 %shard_map.105 = bf16[8,2,32,512]{3,2,1,0:T(8,128)(2,1)} custom-call(s32[20]{0:T(128)S(1)} %pad_add_fusion.plan, bf16[8,2,32,576]{3,2,1,0:T(8,128)(2,1)S(1)} %bitcast.24, bf16[192,1152]{1,0:T(8,128)(2,1)S(1)} %bitcast.25, bf16[2,16,576]{2,1,0:T(8,128)(2,1)S(1)} %pad.4.own), custom_call_target="tpu_custom_call" | custom-call | tf_op jit(solution)/shard_map/pallas_call | solution.py:117
  69.1 4.0 %all-to-all-start.2 = ((bf16[1,1,16,2,16,512]{5,4,3,1,0,2:T(8,128)(2,1)}), bf16[1,1,16,2,16,512]{5,4,3,1,0,2:T(8,128)(2,1)S(1)}, u32[]{:S(2)}, u32[]{:S(2)}) async-start(bf16[1,1,16,2,16,512]{5,4,3,1,0,2:T(8,128)(2,1)} %bitcast.8), calls=%async_computation.2 | async-start | bytes 1048576 | tf_op jit(solution)/shard_map/all_to_all | solution.py:230
  73.2 0.0 copy-start.1
  73.2 2.0 %copy-done.1 = bf16[1,1,3,1024,576]{3,4,2,1,0:T(8,128)(2,1)S(1)} copy-done((bf16[1,1,3,1024,576]{3,4,2,1,0:T(8,128)(2,1)S(1)}, bf16[1,1,3,1024,576]{3,4,2,1,0:T(8,128)(2,1)}, u32[]{:S(2)}) %copy-start.1) | copy-done | bytes 3538968
  75.2 3.2 %shard_map.106 = bf16[3,32,512]{2,1,0:T(8,128)(2,1)} custom-call(s32[3]{0:T(128)S(1)} %bitcast.28, bf16[3,32,576]{2,1,0:T(8,128)(2,1)S(1)} %bitcast.26, bf16[3,576,1024]{2,1,0:T(8,128)(2,1)S(1)} %bitcast.23, bf16[3,2,576]{2,1,0:T(2,128)(2,1)S(1)} %bitcast.27), custom_call_target="tpu_custom_call" | custom-call | tf_op jit(solution)/shard_map/pallas_call | solution.py:117
  78.5 10.2 %all-to-all-done.2 = bf16[1,1,16,2,16,512]{5,4,3,1,0,2:T(8,128)(2,1)S(1)} async-done(((bf16[1,1,16,2,16,512]{5,4,3,1,0,2:T(8,128)(2,1)}), bf16[1,1,16,2,16,512]{5,4,3,1,0,2:T(8,128)(2,1)S(1)}, u32[]{:S(2)}, u32[]{:S(2)}) %all-to-all-start.2) | async-done | bytes 524320 | tf_op jit(solution)/shard_map/all_to_all | solution.py:230
  88.6 0.8 copy.25
  (16 shorter events, 0.1 us)
Async XLA Ops:
  0.6 18.2 %copy-start = (bf16[1,1,16,2,576]{4,3,2,1,0:T(2,128)(2,1)S(1)}, bf16[1,1,16,2,576]{4,3,2,1,0:T(2,128)(2,1)}, u32[]{:S(2)}) copy-start(bf16[1,1,16,2,576]{4,3,2,1,0:T(2,128)(2,1)} %param.13) | copy-start | bytes 110596
  0.6 72.5 %copy-start.4 = (s32[1,1,3]{2,1,0:T(1,128)S(1)}, s32[1,1,3]{2,1,0:T(1,128)}, u32[]{:S(2)}) copy-start(s32[1,1,3]{2,1,0:T(1,128)} %param.17) | copy-start | bytes 40
  0.7 72.5 %copy-start.2 = (bf16[1,1,3,2,16,576]{5,4,3,2,1,0:T(8,128)(2,1)S(1)}, bf16[1,1,3,2,16,576]{5,4,3,2,1,0:T(8,128)(2,1)}, u32[]{:S(2)}) copy-start(bf16[1,1,3,2,16,576]{5,4,3,2,1,0:T(8,128)(2,1)} %param.15) | copy-start | bytes 331780
  0.7 72.5 %copy-start.3 = (bf16[1,1,3,2,576]{4,3,2,1,0:T(2,128)(2,1)S(1)}, bf16[1,1,3,2,576]{4,3,2,1,0:T(2,128)(2,1)}, u32[]{:S(2)}) copy-start(bf16[1,1,3,2,576]{4,3,2,1,0:T(2,128)(2,1)} %param.16) | copy-start | bytes 20740
  0.7 44.7 %all-to-all-start = ((bf16[16,2,16,576]{3,2,1,0:T(8,128)(2,1)}), bf16[16,2,16,576]{3,2,1,0:T(8,128)(2,1)S(1)}, u32[]{:S(2)}, u32[]{:S(2)}) async-start(bf16[16,2,16,576]{3,2,1,0:T(8,128)(2,1)} %bitcast.30), calls=%async_computation | async-start | bytes 1310720 | tf_op jit(solution)/shard_map/all_to_all | solution.py:190
  19.1 26.3 %collective-permute-start = (bf16[4,24,576]{2,1,0:T(8,128)(2,1)}, bf16[4,24,576]{2,1,0:T(8,128)(2,1)S(1)}, u32[]{:S(2)}, u32[]{:S(2)}) collective-permute-start(bf16[4,24,576]{2,1,0:T(8,128)(2,1)} %bitcast.33), channel_id=1, source_target_pairs={{0,544},{1,536},{2,528},{3,520},{4,512},{5,568},{6,560},{7,552},{8... | collective-permute-start | bytes 331784 | tf_op jit(solution)/shard_map/ppermute | solution.py:188
  27.7 17.7 %collective-permute-start.1 = (bf16[4,24,576]{2,1,0:T(8,128)(2,1)}, bf16[4,24,576]{2,1,0:T(8,128)(2,1)S(1)}, u32[]{:S(2)}, u32[]{:S(2)}) collective-permute-start(bf16[4,24,576]{2,1,0:T(8,128)(2,1)} %bitcast.34), channel_id=1, source_target_pairs={{0,608},{1,600},{2,592},{3,584},{4,576},{5,632},{6,624},{7,616},{8... | collective-permute-start | bytes 331784 | tf_op jit(solution)/shard_map/ppermute | solution.py:188
  69.1 19.5 %all-to-all-start.2 = ((bf16[1,1,16,2,16,512]{5,4,3,1,0,2:T(8,128)(2,1)}), bf16[1,1,16,2,16,512]{5,4,3,1,0,2:T(8,128)(2,1)S(1)}, u32[]{:S(2)}, u32[]{:S(2)}) async-start(bf16[1,1,16,2,16,512]{5,4,3,1,0,2:T(8,128)(2,1)} %bitcast.8), calls=%async_computation.2 | async-start | bytes 1048576 | tf_op jit(solution)/shard_map/all_to_all | solution.py:230
  73.2 2.0 %copy-start.1 = (bf16[1,1,3,1024,576]{3,4,2,1,0:T(8,128)(2,1)S(1)}, bf16[1,1,3,1024,576]{3,4,2,1,0:T(8,128)(2,1)}, u32[]{:S(2)}) copy-start(bf16[1,1,3,1024,576]{3,4,2,1,0:T(8,128)(2,1)} %param.14) | copy-start | bytes 10616836

commit v4 on v3

--- a/solution.py
+++ b/solution.py
@@ -96,7 +96,7 @@
             [kv[:, j * LATENT : (j + 1) * LATENT], own[j, :, :LATENT]], axis=0
         )
         scores = dot_rows(q[:, :LATENT], latents) + dot_rows(q_rotary, key_rotary)
-        source_chip = (turn + blocks - came_by) % blocks
+        source_chip = (turn + came_by) % blocks
         position = source_chip * chunk + (column - came_by * chunk)
         position = jnp.where(column < cached, position, column - cached)
         bound = jnp.where(column < cached, length, step + 1)
@@ -139,7 +139,7 @@
     pick = jnp.sum(jnp.where(to == target, which, 0), axis=2) + turn[:, :, 0] * prompts
     held = jnp.sum(jnp.where(to[0] == half * ys + here, long[0], 0), axis=1)
     slot = chip * per + lax.broadcasted_iota(jnp.int32, (per,), 0)
-    return jnp.concatenate([pick.reshape(-1), held, (slot + slot // per + 4) % ys])
+    return jnp.concatenate([pick.reshape(-1), held, (slot // per + 4 - slot) % ys])
 
 
 def hand_over_pairs(groups, halves, ys, chips, turn):
@@ -153,7 +153,7 @@
                     to = (
                         (group + groups // 2) % groups,
                         (node + turn) % halves,
-                        (node + node // per + 4 - chip) % ys,
+                        (node - node // per + 4 + chip) % ys,
                         node // per,
                     )
                     pairs.append((

time: 90.5 us -> 95.1 us (1.051)
  blocking collectives: 20.7 us -> 24 us
  waiting for transfers between devices: 17.9 us -> 20.3 us
    all_to_all x1, blocking collectives: 20.7 us -> 24 us  [on_device(): kv = lax.all_to_all(outgoing, 'y', split_axis=0, concat_axis=0, tiled=True)]
    all_to_all x1, waiting for transfers between devices: 7.67 us -> 9.18 us  [on_device(): lax.all_to_all(new_queries[0, 0], 'chip', split_axis=0, concat_axis=0, ti...]
  transfers between devices with their start and end apart: 4 -> 4, of which waited for: 2 -> 2; matrix products, arithmetic and copies ran while one was open for 2% -> 2% of each run, Pallas kernels for 4% -> 3%
where the time goes in v4:
time: 95.1 us; the launch traced here: 94.7 us
  starting transfers between devices  38.9 us (41%)
  blocking collectives  24 us (25%)
  waiting for transfers between devices  20.3 us (21%)
  Pallas kernels  6.29 us (7%)
  local copies, waits for them, and re-layouts  4.03 us (4%)
    all_to_all x1, blocking collectives, on_device(): kv = lax.all_to_all(outgoing, 'y', split_axis=0, concat_axis=0, tiled=True)  24 us
    ppermute x2, starting transfers between devices, on_device(): lax.ppermute(prompt_cache[0, 0], axes, hand_over_pairs(*sizes, turn))  18.6 us
    all_to_all x1, starting transfers between devices, on_device(): lax.all_to_all(new_queries[0, 0], 'chip', split_axis=0, concat_axis=0, ti...  16.8 us
    all_to_all x1, waiting for transfers between devices, on_device(): lax.all_to_all(context, 'chip', split_axis=2, concat_axis=2, tiled=True)  11.1 us
    all_to_all x1, waiting for transfers between devices, on_device(): lax.all_to_all(new_queries[0, 0], 'chip', split_axis=0, concat_axis=0, ti...  9.18 us
    pallas_call x3, Pallas kernels, call(): pl.pallas_call(kernel, out_shape=jax.ShapeDtypeStruct(shape, jnp.bfloat16...  6.29 us
    all_to_all x1, starting transfers between devices, on_device(): lax.all_to_all(context, 'chip', split_axis=2, concat_axis=2, tiled=True)  3.51 us
    unnamed x11, local copies, waits for them, and re-layouts  2.81 us
  transfers between devices with their start and end apart: 4, of which 2 were waited for; matrix products, arithmetic and copies ran while one was open for 2% of the time, Pallas kernels for 3%

profile of v4, /device:TPU:14, one launch (start us, length us, event | category | flops | bytes accessed | tf_op | source)
XLA Modules:
  0.0 94.7 jit_solution(11978842352970060288)
XLA Ops:
  0.6 0.0 copy-start
  0.7 16.8 %all-to-all-start = ((bf16[16,2,16,576]{3,2,1,0:T(8,128)(2,1)}), bf16[16,2,16,576]{3,2,1,0:T(8,128)(2,1)S(1)}, u32[]{:S(2)}, u32[]{:S(2)}) async-start(bf16[16,2,16,576]{3,2,1,0:T(8,128)(2,1)} %bitcast.30), calls=%async_computation | async-start | bytes 1310720 | tf_op jit(solution)/shard_map/all_to_all | solution.py:190
  17.5 0.8 constant_dynamic-slice_fusion
  18.3 0.1 copy.19
  18.4 0.1 select_reduce_fusion
  18.5 0.1 copy.20
  18.5 0.1 reduce_sum.21
  18.7 0.1 mul.19
  18.8 0.1 copy.21
  18.9 0.1 fusion
  19.0 0.1 pad_add_fusion.plan
  19.1 8.6 %collective-permute-start = (bf16[4,24,576]{2,1,0:T(8,128)(2,1)}, bf16[4,24,576]{2,1,0:T(8,128)(2,1)S(1)}, u32[]{:S(2)}, u32[]{:S(2)}) collective-permute-start(bf16[4,24,576]{2,1,0:T(8,128)(2,1)} %bitcast.33), channel_id=1, source_target_pairs={{0,544},{1,552},{2,560},{3,568},{4,512},{5,520},{6,528},{7,536},{8... | collective-permute-start | bytes 331784 | tf_op jit(solution)/shard_map/ppermute | solution.py:188
  27.7 10.0 %collective-permute-start.1 = (bf16[4,24,576]{2,1,0:T(8,128)(2,1)}, bf16[4,24,576]{2,1,0:T(8,128)(2,1)S(1)}, u32[]{:S(2)}, u32[]{:S(2)}) collective-permute-start(bf16[4,24,576]{2,1,0:T(8,128)(2,1)} %bitcast.34), channel_id=1, source_target_pairs={{0,608},{1,616},{2,624},{3,632},{4,576},{5,584},{6,592},{7,600},{8... | collective-permute-start | bytes 331784 | tf_op jit(solution)/shard_map/ppermute | solution.py:188
  37.7 9.2 %all-to-all-done = bf16[16,2,16,576]{3,2,1,0:T(8,128)(2,1)S(1)} async-done(((bf16[16,2,16,576]{3,2,1,0:T(8,128)(2,1)}), bf16[16,2,16,576]{3,2,1,0:T(8,128)(2,1)S(1)}, u32[]{:S(2)}, u32[]{:S(2)}) %all-to-all-start) | async-done | bytes 589856 | tf_op jit(solution)/shard_map/all_to_all | solution.py:190
  46.9 0.0 collective-permute-done.first
  46.9 0.7 shard_map.104
  47.6 24.0 %all_to_all.15 = bf16[8,24,1152]{2,1,0:T(8,128)(2,1)S(1)} all-to-all(bf16[8,24,1152]{2,1,0:T(8,128)(2,1)S(1)} %shard_map.104), channel_id=1, replica_groups=mesh['group'=8,'xh'=2,'y'=8,'chip'=8] {'y'}, dimensions={0} | all-to-all | bytes 884736 | tf_op jit(solution)/shard_map/all_to_all | solution.py:213
  71.6 2.4 %shard_map.105 = bf16[8,2,32,512]{3,2,1,0:T(8,128)(2,1)} custom-call(s32[20]{0:T(128)S(1)} %pad_add_fusion.plan, bf16[8,2,32,576]{3,2,1,0:T(8,128)(2,1)S(1)} %bitcast.24, bf16[192,1152]{1,0:T(8,128)(2,1)S(1)} %bitcast.25, bf16[2,16,576]{2,1,0:T(8,128)(2,1)S(1)} %pad.4.own), custom_call_target="tpu_custom_call" | custom-call | tf_op jit(solution)/shard_map/pallas_call | solution.py:117
  74.0 3.5 %all-to-all-start.2 = ((bf16[1,1,16,2,16,512]{5,4,3,1,0,2:T(8,128)(2,1)}), bf16[1,1,16,2,16,512]{5,4,3,1,0,2:T(8,128)(2,1)S(1)}, u32[]{:S(2)}, u32[]{:S(2)}) async-start(bf16[1,1,16,2,16,512]{5,4,3,1,0,2:T(8,128)(2,1)} %bitcast.8), calls=%async_computation.2 | async-start | bytes 1048576 | tf_op jit(solution)/shard_map/all_to_all | solution.py:230
  77.5 0.0 copy-start.1
  77.6 2.0 %copy-done.1 = bf16[1,1,3,1024,576]{3,4,2,1,0:T(8,128)(2,1)S(1)} copy-done((bf16[1,1,3,1024,576]{3,4,2,1,0:T(8,128)(2,1)S(1)}, bf16[1,1,3,1024,576]{3,4,2,1,0:T(8,128)(2,1)}, u32[]{:S(2)}) %copy-start.1) | copy-done | bytes 3538968
  79.6 3.2 %shard_map.106 = bf16[3,32,512]{2,1,0:T(8,128)(2,1)} custom-call(s32[3]{0:T(128)S(1)} %bitcast.28, bf16[3,32,576]{2,1,0:T(8,128)(2,1)S(1)} %bitcast.26, bf16[3,576,1024]{2,1,0:T(8,128)(2,1)S(1)} %bitcast.23, bf16[3,2,576]{2,1,0:T(2,128)(2,1)S(1)} %bitcast.27), custom_call_target="tpu_custom_call" | custom-call | tf_op jit(solution)/shard_map/pallas_call | solution.py:117
  82.8 11.1 %all-to-all-done.2 = bf16[1,1,16,2,16,512]{5,4,3,1,0,2:T(8,128)(2,1)S(1)} async-done(((bf16[1,1,16,2,16,512]{5,4,3,1,0,2:T(8,128)(2,1)}), bf16[1,1,16,2,16,512]{5,4,3,1,0,2:T(8,128)(2,1)S(1)}, u32[]{:S(2)}, u32[]{:S(2)}) %all-to-all-start.2) | async-done | bytes 524320 | tf_op jit(solution)/shard_map/all_to_all | solution.py:230
  93.9 0.8 copy.25
  (16 shorter events, 0.1 us)
Async XLA Ops:
  0.6 18.2 %copy-start = (bf16[1,1,16,2,576]{4,3,2,1,0:T(2,128)(2,1)S(1)}, bf16[1,1,16,2,576]{4,3,2,1,0:T(2,128)(2,1)}, u32[]{:S(2)}) copy-start(bf16[1,1,16,2,576]{4,3,2,1,0:T(2,128)(2,1)} %param.13) | copy-start | bytes 110596
  0.6 76.9 %copy-start.4 = (s32[1,1,3]{2,1,0:T(1,128)S(1)}, s32[1,1,3]{2,1,0:T(1,128)}, u32[]{:S(2)}) copy-start(s32[1,1,3]{2,1,0:T(1,128)} %param.17) | copy-start | bytes 40
  0.7 76.9 %copy-start.2 = (bf16[1,1,3,2,16,576]{5,4,3,2,1,0:T(8,128)(2,1)S(1)}, bf16[1,1,3,2,16,576]{5,4,3,2,1,0:T(8,128)(2,1)}, u32[]{:S(2)}) copy-start(bf16[1,1,3,2,16,576]{5,4,3,2,1,0:T(8,128)(2,1)} %param.15) | copy-start | bytes 331780
  0.7 76.9 %copy-start.3 = (bf16[1,1,3,2,576]{4,3,2,1,0:T(2,128)(2,1)S(1)}, bf16[1,1,3,2,576]{4,3,2,1,0:T(2,128)(2,1)}, u32[]{:S(2)}) copy-start(bf16[1,1,3,2,576]{4,3,2,1,0:T(2,128)(2,1)} %param.16) | copy-start | bytes 20740
  0.7 46.2 %all-to-all-start = ((bf16[16,2,16,576]{3,2,1,0:T(8,128)(2,1)}), bf16[16,2,16,576]{3,2,1,0:T(8,128)(2,1)S(1)}, u32[]{:S(2)}, u32[]{:S(2)}) async-start(bf16[16,2,16,576]{3,2,1,0:T(8,128)(2,1)} %bitcast.30), calls=%async_computation | async-start | bytes 1310720 | tf_op jit(solution)/shard_map/all_to_all | solution.py:190
  19.1 27.8 %collective-permute-start = (bf16[4,24,576]{2,1,0:T(8,128)(2,1)}, bf16[4,24,576]{2,1,0:T(8,128)(2,1)S(1)}, u32[]{:S(2)}, u32[]{:S(2)}) collective-permute-start(bf16[4,24,576]{2,1,0:T(8,128)(2,1)} %bitcast.33), channel_id=1, source_target_pairs={{0,544},{1,552},{2,560},{3,568},{4,512},{5,520},{6,528},{7,536},{8... | collective-permute-start | bytes 331784 | tf_op jit(solution)/shard_map/ppermute | solution.py:188
  27.7 19.2 %collective-permute-start.1 = (bf16[4,24,576]{2,1,0:T(8,128)(2,1)}, bf16[4,24,576]{2,1,0:T(8,128)(2,1)S(1)}, u32[]{:S(2)}, u32[]{:S(2)}) collective-permute-start(bf16[4,24,576]{2,1,0:T(8,128)(2,1)} %bitcast.34), channel_id=1, source_target_pairs={{0,608},{1,616},{2,624},{3,632},{4,576},{5,584},{6,592},{7,600},{8... | collective-permute-start | bytes 331784 | tf_op jit(solution)/shard_map/ppermute | solution.py:188
  74.0 19.9 %all-to-all-start.2 = ((bf16[1,1,16,2,16,512]{5,4,3,1,0,2:T(8,128)(2,1)}), bf16[1,1,16,2,16,512]{5,4,3,1,0,2:T(8,128)(2,1)S(1)}, u32[]{:S(2)}, u32[]{:S(2)}) async-start(bf16[1,1,16,2,16,512]{5,4,3,1,0,2:T(8,128)(2,1)} %bitcast.8), calls=%async_computation.2 | async-start | bytes 1048576 | tf_op jit(solution)/shard_map/all_to_all | solution.py:230
  77.5 2.0 %copy-start.1 = (bf16[1,1,3,1024,576]{3,4,2,1,0:T(8,128)(2,1)S(1)}, bf16[1,1,3,1024,576]{3,4,2,1,0:T(8,128)(2,1)}, u32[]{:S(2)}) copy-start(bf16[1,1,3,1024,576]{3,4,2,1,0:T(8,128)(2,1)} %param.14) | copy-start | bytes 10616836
